TPU v7x, 128 devices: a whole 4x4x4 slice. The times are simulated.
128 devices in a mesh: view: 2 (over z_lo), dp: 64 (over y, z_hi, x, core).
Axes of the slice: x: 4, y: 4, z: 4 (z_hi: 2, z_lo: 2; z = z_hi * 2 + z_lo), core: 2. Of those that a mesh axis runs over, the one named last changes fastest.
Arguments:
- hidden: bfloat16 [2, 896, 4096], P('view', 'dp')
- weight: bfloat16 [4096, 8192], P(None, 'dp')
Outputs:
- grad_hidden: float32 [2, 896, 4096], P('view', 'dp')
- grad_weight: float32 [4096, 8192], P(None, 'dp')
All inputs are finite; a program needn't handle non-finite values.
Results may differ from a plain program's by a relative error of at most 0.003.
Values may be sent and summed in bfloat16 or wider, within the bound.
No kernel may reach another device: no remote copies, remote signals or barrier semaphores. Data moves between devices by JAX's collectives and lax.ppermute only.
A program may use at most 128 MiB of HBM per device.

v0:
```python
import jax
import jax.numpy as jnp
from jax import lax
from jax.sharding import PartitionSpec as P


def from_partner(block, axis, apart):
    count = lax.axis_size(axis)
    route = []
    for low in range(count):
        high = low | 1 << apart
        if high != low and high < count:
            route += [(low, high), (high, low)]
    return lax.ppermute(block, axis, route)


def split_parts(values):
    upper = values.astype(jnp.bfloat16)
    lower = (values - upper.astype(jnp.float32)).astype(jnp.bfloat16)
    return (upper, lower)


def coupling_term(centered):
    segment = lax.all_gather(centered, "dp", axis=1, tiled=True)
    product_tile = lax.dot_general(
        centered, segment, (((0,), (0,)), ((), ())), preferred_element_type=jnp.float32
    )
    tile_upper, tile_lower = split_parts(product_tile)
    dims = (((1,), (1,)), ((), ()))
    running = lax.dot_general(segment, tile_upper, dims, preferred_element_type=jnp.float32)
    return running + lax.dot_general(segment, tile_lower, dims, preferred_element_type=jnp.float32)


def view_gradient(embedded, partner, weight):
    total_rows = embedded.shape[0]
    embed_wide = embedded.astype(jnp.float32)
    centered = (embed_wide - jnp.mean(embed_wide, axis=0, keepdims=True)).astype(jnp.bfloat16)
    centered_wide = centered.astype(jnp.float32)
    sum_squares = jnp.sum(centered_wide * centered_wide, axis=0, keepdims=True)
    spread_std = jnp.sqrt(sum_squares / (total_rows - 1) + 0.0001)
    coupled = coupling_term(centered)
    coef_var = total_rows / (2.0 * (total_rows - 1))
    coef_cov = 0.08 * total_rows / ((total_rows - 1) * (total_rows - 1))
    hinge_weight = jax.nn.sigmoid(10.0 * (1.0 - spread_std))
    combined = (
        embed_wide
        - partner.astype(jnp.float32)
        - coef_var * hinge_weight * centered_wide / spread_std
    )
    combined = combined + coef_cov * (coupled - centered_wide * sum_squares)
    grad_embed = combined.astype(jnp.bfloat16)
    grad_rows = lax.psum_scatter(
        lax.dot_general(
            grad_embed, weight, (((1,), (1,)), ((), ())), preferred_element_type=jnp.float32
        ),
        "dp",
        scatter_dimension=0,
        tiled=True,
    )
    return (grad_embed, grad_rows)


def on_device(hidden, weight):
    local_views = hidden.shape[0]
    gathered = lax.all_gather(hidden, "dp", axis=1, tiled=True)
    total_rows = gathered.shape[1]
    in_width = gathered.shape[2]
    flat = gathered.reshape(local_views * total_rows, in_width)
    embedded = jnp.dot(flat, weight, preferred_element_type=jnp.float32).astype(jnp.bfloat16)
    embedded = embedded.reshape(local_views, total_rows, weight.shape[1])
    partners = from_partner(embedded, "view", 0)
    grad_embed, grad_rows = view_gradient(embedded[0], partners[0], weight)
    grad_list = [grad_rows]
    weight_part = lax.dot_general(
        gathered[0], grad_embed, (((0,), (0,)), ((), ())), preferred_element_type=jnp.float32
    )
    grad_weight = lax.psum(weight_part, "view") / jnp.sqrt(2.0 * total_rows)
    return (jnp.stack(grad_list), grad_weight)


def solution(mesh):
    return jax.shard_map(
        on_device,
        mesh=mesh,
        in_specs=(P("view", "dp", None), P(None, "dp")),
        out_specs=(P("view", "dp", None), P(None, "dp")),
        check_vma=False,
    )
```

profile of v0, /device:TPU:8, one launch (start us, length us, event | category | flops | bytes accessed | tf_op | source)
XLA Modules:
  0.0 558.8 jit_solution(7315536405936615213)
XLA Ops:
  7.2 1.9 copy.9
  9.1 0.0 all-gather.5.cloned.1.call-start
  9.2 105.2 %all-gather.3.cloned.1.call-done = bf16[1,896,4096]{2,0,1:T(2,128)(2,1)} async-done(((bf16[1,14,4096]{2,0,1:T(2,128)(2,1)}), bf16[1,896,4096]{2,0,1:T(2,128)(2,1)}) %all-gather.3.cloned.1.call-update) | async-done | bytes 7340048 | tf_op jit(solution)/shard_map/all_gather | solution.py:65
  114.3 12.9 %convert_reduce_fusion = (f32[128]{0:T(128)S(1)}, bf16[896,128]{1,0:T(8,128)(2,1)S(1)}) fusion(bf16[4096,128]{1,0:T(8,128)(2,1)S(1)} %copy-done, bf16[1,896,4096]{2,0,1:T(2,128)(2,1)} %all-gather.3.cloned.1.call-done), kind=kOutput, calls=%fused_computation.21 | convolution fusion | flops 939868032 | bytes 8618496 | tf_op jit(solution)/shard_map/dot_general | solution.py:69
  127.3 0.8 fusion.24
  128.1 0.9 collective-permute-start
  129.1 130.5 %all-gather.5.cloned.1.call-done = bf16[896,8192]{1,0:T(8,128)(2,1)} async-done(((bf16[896,128]{1,0:T(8,128)(2,1)}), bf16[896,8192]{1,0:T(8,128)(2,1)}) %all-gather.5.cloned.1.call-update) | async-done | bytes 14680080 | tf_op jit(solution)/shard_map/all_gather | solution.py:24
  259.6 8.0 %fusion.26 = f32[128,8192]{1,0:T(8,128)S(1)} fusion(bf16[896,8192]{1,0:T(8,128)(2,1)} %all-gather.5.cloned.1.call-done, bf16[896,128]{1,0:T(8,128)(2,1)S(1)} %get-tuple-element.13, f32[128]{0:T(128)S(1)} %broadcast_multiply_fusion.1), kind=kOutput, calls=%fused_computation.30 | convolution fusion | flops 1879392256 | bytes 19104256 | tf_op jit(solution)/shard_map/dot_general | solution.py:25
  267.6 1.4 copy-done.1
  268.9 3.9 fusion.18
  272.9 4.2 fusion.22
  277.1 7.5 %fusion.28 = f32[896,4096]{1,0:T(8,128)} fusion(bf16[896,128]{1,0:T(8,128)(2,1)S(1)} %fusion.22, bf16[4096,128]{1,0:T(8,128)(2,1)S(1)} %copy-done), kind=kOutput, calls=%fused_computation.34 | convolution fusion | flops 939524096 | bytes 15958016 | tf_op jit(solution)/shard_map/dot_general | solution.py:53
  284.6 14.8 %fusion.5 = f32[4096,128]{0,1:T(8,128)} fusion(bf16[896,128]{1,0:T(8,128)(2,1)S(1)} %fusion.22, bf16[1,896,4096]{2,0,1:T(2,128)(2,1)} %all-gather.3.cloned.1.call-done), kind=kOutput, calls=%fused_computation.4 | convolution fusion | flops 939524096 | bytes 9666560 | tf_op jit(solution)/shard_map/dot_general | solution.py:74
  299.5 171.8 %fusion = f32[16,4096]{1,0:T(8,128)S(1)} fusion(f32[896,4096]{1,0:T(8,128)} %fusion.28), kind=kCustom, calls=%all-reduce-scatter | all-reduce-scatter fusion | flops 4194305 | bytes 14942720
  471.3 1.9 collective-permute-start.1
  473.2 1.9 collective-permute-start.2
  475.2 1.9 collective-permute-start.8
  477.1 1.9 collective-permute-start.3
  479.0 9.9 %collective-permute-start.4 = (f32[16,4096]{1,0:T(8,128)S(1)}, f32[16,4096]{1,0:T(8,128)S(1)}, u32[]{:S(2)}, u32[]{:S(2)}) collective-permute-start(f32[16,4096]{1,0:T(8,128)S(1)} %fusion), channel_id=1, source_target_pairs={{0,4},{1,5},{2,6},{3,7},{4,8},{5,9},{6,10},{7,11},{8,12},{9,13},{1... | collective-permute-start | bytes 786440
  488.9 16.9 %collective-permute-done.8 = f32[14,4096]{1,0:T(8,128)S(1)} collective-permute-done((f32[14,4096]{1,0:T(8,128)S(1)}, f32[14,4096]{1,0:T(8,128)S(1)}, u32[]{:S(2)}, u32[]{:S(2)}) %collective-permute-start.8) | collective-permute-done | bytes 229408
  505.8 1.9 collective-permute-start.5
  507.7 1.9 collective-permute-start.6
  509.7 1.9 collective-permute-start.7
  511.7 0.6 dynamic-slice.4
  512.9 6.1 %collective-permute-done.5 = f32[16,4096]{1,0:T(8,128)S(1)} collective-permute-done((f32[16,4096]{1,0:T(8,128)S(1)}, f32[16,4096]{1,0:T(8,128)S(1)}, u32[]{:S(2)}, u32[]{:S(2)}) %collective-permute-start.5) | collective-permute-done | bytes 262176
  519.0 6.1 %collective-permute-done.6 = f32[16,4096]{1,0:T(8,128)S(1)} collective-permute-done((f32[16,4096]{1,0:T(8,128)S(1)}, f32[16,4096]{1,0:T(8,128)S(1)}, u32[]{:S(2)}, u32[]{:S(2)}) %collective-permute-start.6) | collective-permute-done | bytes 262176
  525.1 0.7 copy-done.9
  525.8 5.1 collective-permute-done.7
  530.9 16.7 %concatenate = f32[142,4096]{1,0:T(8,128)S(1)} concatenate(f32[14,4096]{1,0:T(8,128)} %copy-done.5, f32[16,4096]{1,0:T(8,128)} %collective-permute-done.7, f32[16,4096]{1,0:T(8,128)} %copy-done.9, f32[16,4096]{1,0:T(8,128)} %copy-done.8, f32[16,4096]{1,0:T(8,128)} %copy-done.7, f32[16,4096]{1,0:T(8,128)} %copy-done.6, f32[16,4096]{1,0:T(8,128)} %copy-done.4, ...), dimensions={0} | concatenate | bytes 4653056
  547.7 0.9 copy.10
  548.6 1.8 broadcast_multiply_fusion
  550.4 1.8 copy.11
  (35 shorter events, 0.3 us)
Async XLA Ops:
  7.2 107.2 %copy-start = (bf16[4096,128]{1,0:T(8,128)(2,1)S(1)}, bf16[4096,128]{1,0:T(8,128)(2,1)}, u32[]{:S(2)}) copy-start(bf16[4096,128]{1,0:T(8,128)(2,1)} %param.3) | copy-start | bytes 3145732
  7.2 107.2 %all-gather.3.cloned.1.call-start = ((), (), s32[]{:S(2)}) async-start(), calls=%async_computation | async-start | bytes 14909440 | tf_op jit(solution)/shard_map/all_gather | solution.py:65
  9.1 250.5 %all-gather.5.cloned.1.call-start = ((), (), s32[]{:S(2)}) async-start(), calls=%async_computation.1 | async-start | bytes 14909440 | tf_op jit(solution)/shard_map/all_gather | solution.py:24
  128.1 420.6 %all-reduce.4.cloned.1.call-start = ((), (), s32[]{:S(2)}) async-start(), calls=%async_computation.2 | async-start | bytes 4194304 | tf_op jit(solution)/shard_map/psum | solution.py:77
  128.1 144.8 %collective-permute-start = (bf16[1,896,128]{2,1,0:T(8,128)(2,1)S(1)}, bf16[1,896,128]{2,1,0:T(8,128)(2,1)S(1)}, u32[]{:S(2)}, u32[]{:S(2)}) collective-permute-start(bf16[1,896,128]{2,1,0:T(8,128)(2,1)S(1)} %bitcast.29), channel_id=1, source_target_pairs={{0,64},{64,0},{1,65},{65,1},{2,66},{66,2},{3,67},{67,3},{4,68},{68... | collective-permute-start | bytes 688136 | tf_op jit(solution)/shard_map/ppermute | solution.py:14
  259.6 9.3 %copy-start.1 = (bf16[896,8192]{1,0:T(8,128)(2,1)S(1)}, bf16[896,8192]{1,0:T(8,128)(2,1)}, u32[]{:S(2)}) copy-start(bf16[896,8192]{1,0:T(8,128)(2,1)} %all-gather.5.cloned.1.call-done) | copy-start | bytes 44040196
  299.4 212.2 %copy-start.10 = (u32[128]{0:T(128)S(1)}, u32[128]{0:T(128)}, u32[]{:S(2)}) copy-start(u32[128]{0:T(128)} %constant.24) | copy-start | bytes 1540
  471.3 53.8 %copy-start.2 = (f32[16,4096]{1,0:T(8,128)}, f32[16,4096]{1,0:T(8,128)S(1)}, u32[]{:S(2)}) copy-start(f32[16,4096]{1,0:T(8,128)S(1)} %fusion) | copy-start | bytes 786436
  471.3 36.4 %collective-permute-start.1 = (f32[16,4096]{1,0:T(8,128)S(1)}, f32[16,4096]{1,0:T(8,128)S(1)}, u32[]{:S(2)}, u32[]{:S(2)}) collective-permute-start(f32[16,4096]{1,0:T(8,128)S(1)} %fusion), channel_id=1, source_target_pairs={{0,1},{1,2},{2,3},{3,4},{4,5},{5,6},{6,7},{7,8},{8,9},{9,10},{10,1... | collective-permute-start | bytes 786440
  473.2 36.5 %collective-permute-start.2 = (f32[16,4096]{1,0:T(8,128)S(1)}, f32[16,4096]{1,0:T(8,128)S(1)}, u32[]{:S(2)}, u32[]{:S(2)}) collective-permute-start(f32[16,4096]{1,0:T(8,128)S(1)} %fusion), channel_id=1, source_target_pairs={{0,2},{1,3},{2,4},{3,5},{4,6},{5,7},{6,8},{7,9},{8,10},{9,11},{10,... | collective-permute-start | bytes 786440
  475.2 30.6 %collective-permute-start.8 = (f32[14,4096]{1,0:T(8,128)S(1)}, f32[14,4096]{1,0:T(8,128)S(1)}, u32[]{:S(2)}, u32[]{:S(2)}) collective-permute-start(f32[14,4096]{1,0:T(8,128)S(1)} %slice), channel_id=1, source_target_pairs={{0,8},{1,9},{2,10},{3,11},{4,12},{5,13},{6,14},{7,15},{8,16},{9,17... | collective-permute-start | bytes 688136
  477.1 35.8 %collective-permute-start.3 = (f32[16,4096]{1,0:T(8,128)S(1)}, f32[16,4096]{1,0:T(8,128)S(1)}, u32[]{:S(2)}, u32[]{:S(2)}) collective-permute-start(f32[16,4096]{1,0:T(8,128)S(1)} %fusion), channel_id=1, source_target_pairs={{0,3},{1,4},{2,5},{3,6},{4,7},{5,8},{6,9},{7,10},{8,11},{9,12},{10... | collective-permute-start | bytes 786440
  479.0 33.9 %collective-permute-start.4 = (f32[16,4096]{1,0:T(8,128)S(1)}, f32[16,4096]{1,0:T(8,128)S(1)}, u32[]{:S(2)}, u32[]{:S(2)}) collective-permute-start(f32[16,4096]{1,0:T(8,128)S(1)} %fusion), channel_id=1, source_target_pairs={{0,4},{1,5},{2,6},{3,7},{4,8},{5,9},{6,10},{7,11},{8,12},{9,13},{1... | collective-permute-start | bytes 786440
  505.8 5.8 %copy-start.5 = (f32[14,4096]{1,0:T(8,128)}, f32[14,4096]{1,0:T(8,128)S(1)}, u32[]{:S(2)}) copy-start(f32[14,4096]{1,0:T(8,128)S(1)} %collective-permute-done.8) | copy-start | bytes 688132
  505.8 13.2 %collective-permute-start.5 = (f32[16,4096]{1,0:T(8,128)S(1)}, f32[16,4096]{1,0:T(8,128)S(1)}, u32[]{:S(2)}, u32[]{:S(2)}) collective-permute-start(f32[16,4096]{1,0:T(8,128)S(1)} %fusion), channel_id=1, source_target_pairs={{0,5},{1,6},{2,7},{3,8},{4,9},{5,10},{6,11},{7,12},{8,13},{9,14},{... | collective-permute-start | bytes 786440
  507.7 2.0 copy-start.3
  507.7 17.4 %collective-permute-start.6 = (f32[16,4096]{1,0:T(8,128)S(1)}, f32[16,4096]{1,0:T(8,128)S(1)}, u32[]{:S(2)}, u32[]{:S(2)}) collective-permute-start(f32[16,4096]{1,0:T(8,128)S(1)} %fusion), channel_id=1, source_target_pairs={{0,6},{1,7},{2,8},{3,9},{4,10},{5,11},{6,12},{7,13},{8,14},{9,15},... | collective-permute-start | bytes 786440
  509.7 2.0 copy-start.4
  509.7 21.2 %collective-permute-start.7 = (f32[16,4096]{1,0:T(8,128)S(1)}, f32[16,4096]{1,0:T(8,128)}, u32[]{:S(2)}, u32[]{:S(2)}) collective-permute-start(f32[16,4096]{1,0:T(8,128)S(1)} %fusion), channel_id=1, source_target_pairs={{0,7},{1,8},{2,9},{3,10},{4,11},{5,12},{6,13},{7,14},{8,15},{9,16}... | collective-permute-start | bytes 786440
  512.9 12.2 %copy-start.6 = (f32[16,4096]{1,0:T(8,128)}, f32[16,4096]{1,0:T(8,128)S(1)}, u32[]{:S(2)}) copy-start(f32[16,4096]{1,0:T(8,128)S(1)} %collective-permute-done.3) | copy-start | bytes 786436
  512.9 12.2 %copy-start.7 = (f32[16,4096]{1,0:T(8,128)}, f32[16,4096]{1,0:T(8,128)S(1)}, u32[]{:S(2)}) copy-start(f32[16,4096]{1,0:T(8,128)S(1)} %collective-permute-done.4) | copy-start | bytes 786436
  519.0 6.1 %copy-start.8 = (f32[16,4096]{1,0:T(8,128)}, f32[16,4096]{1,0:T(8,128)S(1)}, u32[]{:S(2)}) copy-start(f32[16,4096]{1,0:T(8,128)S(1)} %collective-permute-done.5) | copy-start | bytes 786436
  525.1 0.7 copy-start.9
Sparse Core Ops, SparseCore 0:
  11.7 102.5 all-gather.2
  128.2 131.3 all-gather.4
  299.6 131.1 all-reduce.3
where the time goes:
time: 560 us; the launch traced here: 559 us
  waiting for transfers between devices  270 us (48%)
  blocking collectives  172 us (31%)
  matrix products  51.4 us (9%)
  starting transfers between devices  24.3 us (4%)
  local copies, waits for them, and re-layouts  24.1 us (4%)
  between operations  14.7 us (3%)
    unnamed x1, blocking collectives  172 us
    all_gather x1, waiting for transfers between devices, coupling_term(): segment = lax.all_gather(centered, 'dp', axis=1, tiled=True)  131 us
    all_gather x1, waiting for transfers between devices, on_device(): gathered = lax.all_gather(hidden, 'dp', axis=1, tiled=True)  105 us
    unnamed x11, waiting for transfers between devices  34.2 us
    unnamed x28, local copies, waits for them, and re-layouts  24.1 us
    unnamed x8, starting transfers between devices  23.3 us
    dot_general x1, matrix products, on_device(): lax.dot_general(gathered[0], grad_embed, (((0,), (0,)), ((), ())), prefer...  14.8 us
    dot_general x1, matrix products, on_device(): jnp.dot(flat, weight, preferred_element_type=jnp.float32)  12.9 us
  transfers between devices with their start and end apart: 12, of which 6 were waited for; matrix products, arithmetic and copies ran while one was open for 36% of the time, Pallas kernels for 0%

commit v1 on v0

--- a/solution.py
+++ b/solution.py
@@ -2,6 +2,11 @@
 import jax.numpy as jnp
 from jax import lax
 from jax.sharding import PartitionSpec as P
+
+
+def gather_over(x, name, d):
+    stack = jnp.stack([x] * lax.axis_size(name))
+    return jnp.concatenate(lax.all_to_all(stack, name, 0, 0), axis=d)
 
 
 def from_partner(block, axis, apart):
@@ -21,7 +26,7 @@
 
 
 def coupling_term(centered):
-    segment = lax.all_gather(centered, "dp", axis=1, tiled=True)
+    segment = gather_over(centered, "dp", 1)
     product_tile = lax.dot_general(
         centered, segment, (((0,), (0,)), ((), ())), preferred_element_type=jnp.float32
     )

time: 560 us -> 644 us (1.15)
  waiting for transfers between devices: 270 us -> 338 us
    all_to_all x0 -> x1, waiting for transfers between devices: none -> 199 us  [gather_over(): return jnp.concatenate(lax.all_to_all(stack, name, 0, 0), axis=d)]
    all_gather x1 -> x0, waiting for transfers between devices: 131 us -> none  [coupling_term(): segment = lax.all_gather(centered, 'dp', axis=1, tiled=True)]
    another operation x0 -> x1, local copies, waits for them, and re-layouts: none -> 7.34 us  [gather_over(): stack = jnp.stack([x] * lax.axis_size(name))]
    unnamed x28 -> x34, local copies, waits for them, and re-layouts: 24.1 us -> 22.7 us
    unnamed x11 -> x10, waiting for transfers between devices: 34.2 us -> 33.3 us
  transfers between devices with their start and end apart: 12 -> 12, of which waited for: 6 -> 6; matrix products, arithmetic and copies ran while one was open for 36% -> 32% of each run, Pallas kernels for 0% -> 0%
where the time goes in v1:
time: 644 us; the launch traced here: 643 us
  waiting for transfers between devices  338 us (52%)
  blocking collectives  172 us (27%)
  matrix products  55.1 us (9%)
  local copies, waits for them, and re-layouts  30.3 us (5%)
  starting transfers between devices  30.2 us (5%)
  between operations  15 us (2%)
    all_to_all x1, waiting for transfers between devices, gather_over(): return jnp.concatenate(lax.all_to_all(stack, name, 0, 0), axis=d)  199 us
    unnamed x1, blocking collectives  172 us
    all_gather x1, waiting for transfers between devices, on_device(): gathered = lax.all_gather(hidden, 'dp', axis=1, tiled=True)  105 us
    unnamed x10, waiting for transfers between devices  33.3 us
    unnamed x34, local copies, waits for them, and re-layouts  22.7 us
    unnamed x8, starting transfers between devices  22.1 us
    dot_general x1, matrix products, on_device(): jnp.dot(flat, weight, preferred_element_type=jnp.float32)  12.9 us
  transfers between devices with their start and end apart: 12, of which 6 were waited for; matrix products, arithmetic and copies ran while one was open for 32% of the time, Pallas kernels for 0%

profile of v1, /device:TPU:8, one launch (start us, length us, event | category | flops | bytes accessed | tf_op | source)
XLA Modules:
  0.0 642.5 jit_solution(13297689659200285311)
XLA Ops:
  7.2 1.9 copy.13
  9.1 105.2 %all-gather.2.cloned.1.call-done = bf16[1,896,4096]{2,0,1:T(2,128)(2,1)} async-done(((bf16[1,14,4096]{2,0,1:T(2,128)(2,1)}), bf16[1,896,4096]{2,0,1:T(2,128)(2,1)}) %all-gather.2.cloned.1.call-update) | async-done | bytes 7340048 | tf_op jit(solution)/shard_map/all_gather | solution.py:70
  114.3 12.9 %convert_reduce_fusion = (f32[128]{0:T(128)S(1)}, bf16[896,128]{1,0:T(8,128)(2,1)S(1)}) fusion(bf16[4096,128]{1,0:T(8,128)(2,1)S(1)} %copy-done, bf16[1,896,4096]{2,0,1:T(2,128)(2,1)} %all-gather.2.cloned.1.call-done), kind=kOutput, calls=%fused_computation.20 | convolution fusion | flops 939868032 | bytes 8618496 | tf_op jit(solution)/shard_map/dot_general | solution.py:74
  127.4 0.2 copy.14
  127.6 7.3 %stack.4 = bf16[64,896,128]{1,2,0:T(8,128)(2,1)} broadcast(bf16[896,128]{0,1:T(8,128)(2,1)S(1)} %copy.14), dimensions={1,2} | broadcast | bytes 14909440 | tf_op jit(solution)/shard_map/stack | solution.py:8
  134.9 6.4 all-to-all-start
  141.4 1.6 collective-permute-start
  143.1 199.0 %all-to-all-done = bf16[64,896,128]{1,2,0:T(8,128)(2,1)} async-done(((bf16[64,896,128]{1,2,0:T(8,128)(2,1)}), bf16[64,896,128]{1,2,0:T(8,128)(2,1)}, u32[]{:S(2)}, u32[]{:S(2)}) %all-to-all-start) | async-done | bytes 14680096 | tf_op jit(solution)/shard_map/all_to_all | solution.py:9
  342.1 10.0 %fusion.26 = f32[128,8192]{1,0:T(8,128)S(1)} fusion(bf16[896,8192]{0,1:T(8,128)(2,1)} %bitcast.3, bf16[896,128]{1,0:T(8,128)(2,1)S(1)} %get-tuple-element.15, f32[128]{0:T(128)S(1)} %broadcast_multiply_fusion.1), kind=kOutput, calls=%fused_computation.29 | convolution fusion | flops 1879392256 | bytes 19104256 | tf_op jit(solution)/shard_map/dot_general | solution.py:30
  352.1 7.4 %fusion.10 = f32[896,128]{1,0:T(8,128)S(1)} fusion(bf16[896,8192]{0,1:T(8,128)(2,1)} %bitcast.3, f32[128,8192]{1,0:T(8,128)S(1)} %fusion.26), kind=kOutput, calls=%fused_computation.8 | convolution fusion | flops 1883242496 | bytes 19333120 | tf_op jit(solution)/shard_map/dot_general | solution.py:36
  359.5 7.9 %fusion.20 = bf16[896,128]{1,0:T(8,128)(2,1)S(1)} fusion(bf16[896,128]{1,0:T(8,128)(2,1)S(1)} %get-tuple-element.15, bf16[1,896,128]{2,1,0:T(8,128)(2,1)S(1)} %collective-permute-done, f32[896,128]{1,0:T(8,128)S(1)} %fusion.10, bf16[896,8192]{0,1:T(8,128)(2,1)} %bitcast.3, f32[128,8192]{1,0:T(8,128)S(1)} %fusion.26, f32[128]{0:T(128)S(1)} %get-tuple-element.10, ...), kind=kOutput, calls=%fused_computation.24 | convolution fusion | flops 1881817088 | bytes 20023296 | tf_op jit(solution)/shard_map/dot_general | solution.py:35
  367.5 7.2 %fusion.28 = f32[896,4096]{1,0:T(8,128)} fusion(bf16[896,128]{1,0:T(8,128)(2,1)S(1)} %fusion.20, bf16[4096,128]{1,0:T(8,128)(2,1)S(1)} %copy-done), kind=kOutput, calls=%fused_computation.33 | convolution fusion | flops 939524096 | bytes 15958016 | tf_op jit(solution)/shard_map/dot_general | solution.py:58
  374.7 9.6 %fusion.5 = f32[4096,128]{0,1:T(8,128)} fusion(bf16[896,128]{1,0:T(8,128)(2,1)S(1)} %fusion.20, bf16[1,896,4096]{2,0,1:T(2,128)(2,1)S(1)} %bitcast.33), kind=kOutput, calls=%fused_computation.4 | convolution fusion | flops 939524096 | bytes 9666560 | tf_op jit(solution)/shard_map/dot_general | solution.py:79
  384.4 172.4 %fusion = f32[16,4096]{1,0:T(8,128)S(1)} fusion(f32[896,4096]{1,0:T(8,128)} %fusion.28), kind=kCustom, calls=%all-reduce-scatter | all-reduce-scatter fusion | flops 4194305 | bytes 14942720
  556.8 1.9 collective-permute-start.1
  558.7 1.9 collective-permute-start.2
  560.7 1.9 collective-permute-start.8
  562.6 1.9 collective-permute-start.3
  564.6 8.7 %collective-permute-start.4 = (f32[16,4096]{1,0:T(8,128)S(1)}, f32[16,4096]{1,0:T(8,128)S(1)}, u32[]{:S(2)}, u32[]{:S(2)}) collective-permute-start(f32[16,4096]{1,0:T(8,128)S(1)} %fusion), channel_id=1, source_target_pairs={{0,4},{1,5},{2,6},{3,7},{4,8},{5,9},{6,10},{7,11},{8,12},{9,13},{1... | collective-permute-start | bytes 786440
  573.2 16.3 %collective-permute-done.8 = f32[14,4096]{1,0:T(8,128)S(1)} collective-permute-done((f32[14,4096]{1,0:T(8,128)S(1)}, f32[14,4096]{1,0:T(8,128)S(1)}, u32[]{:S(2)}, u32[]{:S(2)}) %collective-permute-start.8) | collective-permute-done | bytes 229408
  589.5 1.9 collective-permute-start.5
  591.5 1.9 collective-permute-start.6
  593.4 1.9 collective-permute-start.7
  595.4 0.6 dynamic-slice.4
  596.7 7.4 %collective-permute-done.5 = f32[16,4096]{1,0:T(8,128)S(1)} collective-permute-done((f32[16,4096]{1,0:T(8,128)S(1)}, f32[16,4096]{1,0:T(8,128)S(1)}, u32[]{:S(2)}, u32[]{:S(2)}) %collective-permute-start.5) | collective-permute-done | bytes 262176
  604.1 3.7 collective-permute-done.6
  607.8 0.7 copy-done.8
  608.5 5.9 collective-permute-done.7
  614.4 16.7 %concatenate = f32[142,4096]{1,0:T(8,128)S(1)} concatenate(f32[14,4096]{1,0:T(8,128)} %copy-done.4, f32[16,4096]{1,0:T(8,128)} %collective-permute-done.7, f32[16,4096]{1,0:T(8,128)} %copy-done.8, f32[16,4096]{1,0:T(8,128)} %copy-done.7, f32[16,4096]{1,0:T(8,128)} %copy-done.6, f32[16,4096]{1,0:T(8,128)} %copy-done.5, f32[16,4096]{1,0:T(8,128)} %copy-done.3, ...), dimensions={0} | concatenate | bytes 4653056
  631.1 0.9 copy.15
  632.1 1.8 broadcast_multiply_fusion
  633.9 1.8 copy.16
  (43 shorter events, 0.4 us)
Async XLA Ops:
  7.2 107.2 %copy-start = (bf16[4096,128]{1,0:T(8,128)(2,1)S(1)}, bf16[4096,128]{1,0:T(8,128)(2,1)}, u32[]{:S(2)}) copy-start(bf16[4096,128]{1,0:T(8,128)(2,1)} %param.3) | copy-start | bytes 3145732
  7.2 107.2 %all-gather.2.cloned.1.call-start = ((), (), s32[]{:S(2)}) async-start(), calls=%async_computation.1 | async-start | bytes 14909440 | tf_op jit(solution)/shard_map/all_gather | solution.py:70
  134.9 207.1 %all-to-all-start = ((bf16[64,896,128]{1,2,0:T(8,128)(2,1)}), bf16[64,896,128]{1,2,0:T(8,128)(2,1)}, u32[]{:S(2)}, u32[]{:S(2)}) async-start(bf16[64,896,128]{1,2,0:T(8,128)(2,1)} %stack.4), calls=%async_computation | async-start | bytes 29360128 | tf_op jit(solution)/shard_map/all_to_all | solution.py:9
  141.4 490.7 %all-reduce.4.cloned.1.call-start = ((), (), s32[]{:S(2)}) async-start(), calls=%async_computation.2 | async-start | bytes 4194304 | tf_op jit(solution)/shard_map/psum | solution.py:82
  141.4 218.0 %collective-permute-start = (bf16[1,896,128]{2,1,0:T(8,128)(2,1)S(1)}, bf16[1,896,128]{2,1,0:T(8,128)(2,1)S(1)}, u32[]{:S(2)}, u32[]{:S(2)}) collective-permute-start(bf16[1,896,128]{2,1,0:T(8,128)(2,1)S(1)} %bitcast.34), channel_id=1, source_target_pairs={{0,64},{64,0},{1,65},{65,1},{2,66},{66,2},{3,67},{67,3},{4,68},{68... | collective-permute-start | bytes 688136 | tf_op jit(solution)/shard_map/ppermute | solution.py:19
  359.5 15.2 %slice-start = ((s8[14680064]{0:T(1024)(128)(4,1)}), s8[4194304]{0:T(1024)(128)(4,1)S(1)}, s32[]{:S(2)}) async-start(s8[14680064]{0:T(1024)(128)(4,1)} %bitcast.32), calls=%async_computation.3 | async-start | bytes 8388608
  359.5 15.2 %slice-start.1 = ((s8[14680064]{0:T(1024)(128)(4,1)}), s8[4194304]{0:T(1024)(128)(4,1)S(1)}, s32[]{:S(2)}) async-start(s8[14680064]{0:T(1024)(128)(4,1)} %bitcast.32), calls=%async_computation.4 | async-start | bytes 8388608
  359.5 15.2 %slice-start.2 = ((s8[14680064]{0:T(1024)(128)(4,1)}), s8[2097152]{0:T(1024)(128)(4,1)S(1)}, s32[]{:S(2)}) async-start(s8[14680064]{0:T(1024)(128)(4,1)} %bitcast.32), calls=%async_computation.5 | async-start | bytes 4194304
  367.5 7.2 %slice-start.3 = ((s8[14680064]{0:T(1024)(128)(4,1)}), s8[4194304]{0:T(1024)(128)(4,1)S(1)}, s32[]{:S(2)}) async-start(s8[14680064]{0:T(1024)(128)(4,1)} %bitcast.32), calls=%async_computation.6 | async-start | bytes 8388608
  384.4 211.0 %copy-start.9 = (u32[128]{0:T(128)S(1)}, u32[128]{0:T(128)}, u32[]{:S(2)}) copy-start(u32[128]{0:T(128)} %constant.24) | copy-start | bytes 1540
  556.8 51.0 %copy-start.1 = (f32[16,4096]{1,0:T(8,128)}, f32[16,4096]{1,0:T(8,128)S(1)}, u32[]{:S(2)}) copy-start(f32[16,4096]{1,0:T(8,128)S(1)} %fusion) | copy-start | bytes 786436
  556.8 34.7 %collective-permute-start.1 = (f32[16,4096]{1,0:T(8,128)S(1)}, f32[16,4096]{1,0:T(8,128)S(1)}, u32[]{:S(2)}, u32[]{:S(2)}) collective-permute-start(f32[16,4096]{1,0:T(8,128)S(1)} %fusion), channel_id=1, source_target_pairs={{0,1},{1,2},{2,3},{3,4},{4,5},{5,6},{6,7},{7,8},{8,9},{9,10},{10,1... | collective-permute-start | bytes 786440
  558.7 34.7 %collective-permute-start.2 = (f32[16,4096]{1,0:T(8,128)S(1)}, f32[16,4096]{1,0:T(8,128)S(1)}, u32[]{:S(2)}, u32[]{:S(2)}) collective-permute-start(f32[16,4096]{1,0:T(8,128)S(1)} %fusion), channel_id=1, source_target_pairs={{0,2},{1,3},{2,4},{3,5},{4,6},{5,7},{6,8},{7,9},{8,10},{9,11},{10,... | collective-permute-start | bytes 786440
  560.7 28.8 %collective-permute-start.8 = (f32[14,4096]{1,0:T(8,128)S(1)}, f32[14,4096]{1,0:T(8,128)S(1)}, u32[]{:S(2)}, u32[]{:S(2)}) collective-permute-start(f32[14,4096]{1,0:T(8,128)S(1)} %slice), channel_id=1, source_target_pairs={{0,8},{1,9},{2,10},{3,11},{4,12},{5,13},{6,14},{7,15},{8,16},{9,17... | collective-permute-start | bytes 688136
  562.6 34.0 %collective-permute-start.3 = (f32[16,4096]{1,0:T(8,128)S(1)}, f32[16,4096]{1,0:T(8,128)S(1)}, u32[]{:S(2)}, u32[]{:S(2)}) collective-permute-start(f32[16,4096]{1,0:T(8,128)S(1)} %fusion), channel_id=1, source_target_pairs={{0,3},{1,4},{2,5},{3,6},{4,7},{5,8},{6,9},{7,10},{8,11},{9,12},{10... | collective-permute-start | bytes 786440
  564.6 32.1 %collective-permute-start.4 = (f32[16,4096]{1,0:T(8,128)S(1)}, f32[16,4096]{1,0:T(8,128)S(1)}, u32[]{:S(2)}, u32[]{:S(2)}) collective-permute-start(f32[16,4096]{1,0:T(8,128)S(1)} %fusion), channel_id=1, source_target_pairs={{0,4},{1,5},{2,6},{3,7},{4,8},{5,9},{6,10},{7,11},{8,12},{9,13},{1... | collective-permute-start | bytes 786440
  589.5 5.8 copy-start.4
  589.5 14.6 %collective-permute-start.5 = (f32[16,4096]{1,0:T(8,128)S(1)}, f32[16,4096]{1,0:T(8,128)S(1)}, u32[]{:S(2)}, u32[]{:S(2)}) collective-permute-start(f32[16,4096]{1,0:T(8,128)S(1)} %fusion), channel_id=1, source_target_pairs={{0,5},{1,6},{2,7},{3,8},{4,9},{5,10},{6,11},{7,12},{8,13},{9,14},{... | collective-permute-start | bytes 786440
  591.5 2.0 copy-start.2
  591.5 16.3 %collective-permute-start.6 = (f32[16,4096]{1,0:T(8,128)S(1)}, f32[16,4096]{1,0:T(8,128)S(1)}, u32[]{:S(2)}, u32[]{:S(2)}) collective-permute-start(f32[16,4096]{1,0:T(8,128)S(1)} %fusion), channel_id=1, source_target_pairs={{0,6},{1,7},{2,8},{3,9},{4,10},{5,11},{6,12},{7,13},{8,14},{9,15},... | collective-permute-start | bytes 786440
  593.4 2.0 copy-start.3
  593.4 20.9 %collective-permute-start.7 = (f32[16,4096]{1,0:T(8,128)S(1)}, f32[16,4096]{1,0:T(8,128)}, u32[]{:S(2)}, u32[]{:S(2)}) collective-permute-start(f32[16,4096]{1,0:T(8,128)S(1)} %fusion), channel_id=1, source_target_pairs={{0,7},{1,8},{2,9},{3,10},{4,11},{5,12},{6,13},{7,14},{8,15},{9,16}... | collective-permute-start | bytes 786440
  596.7 11.1 %copy-start.5 = (f32[16,4096]{1,0:T(8,128)}, f32[16,4096]{1,0:T(8,128)S(1)}, u32[]{:S(2)}) copy-start(f32[16,4096]{1,0:T(8,128)S(1)} %collective-permute-done.3) | copy-start | bytes 786436
  596.7 11.1 %copy-start.6 = (f32[16,4096]{1,0:T(8,128)}, f32[16,4096]{1,0:T(8,128)S(1)}, u32[]{:S(2)}) copy-start(f32[16,4096]{1,0:T(8,128)S(1)} %collective-permute-done.4) | copy-start | bytes 786436
  604.1 3.7 copy-start.7
  607.8 0.7 copy-start.8
Sparse Core Ops, SparseCore 0:
  11.7 102.5 all-gather.1
  384.5 137.7 all-reduce.3
